TPU v7x, 32 devices: a whole 2x2x4 slice. The times are simulated.
32 devices in a mesh: dp: 2 (over y), fsdp: 16 (over z, x, core).
Axes of the slice: x: 2, y: 2, z: 4, core: 2. Of those that a mesh axis runs over, the one named last changes fastest.
Arguments:
- tokens: bfloat16 [16384, 1024], P(('dp', 'fsdp')), may hold values from -6 to 6
- memory: bfloat16 [16384, 1024], P(('dp', 'fsdp')), may hold values from -6 to 6
- cotangent: bfloat16 [16384, 1024], P(('dp', 'fsdp')), may hold values from -6 to 6
- sent_len: int32 [32, 4], P(('dp', 'fsdp')), may hold values from 1 to 256, 512 in all within a row
- mem_len: int32 [32, 4], P(('dp', 'fsdp')), may hold values from 1 to 256, 512 in all within a row
- proj_in: bfloat16 [6, 1024, 1024], P(None, ('dp', 'fsdp')), may hold values from -0.1875 to 0.1875
- proj_out: bfloat16 [2, 1024, 1024], P(None, ('dp', 'fsdp')), may hold values from -2 to 2
- ffn_in: bfloat16 [1024, 4096], P(('dp', 'fsdp')), may hold values from -0.1875 to 0.1875
- ffn_out: bfloat16 [4096, 1024], P(('dp', 'fsdp')), may hold values from -0.375 to 0.375
- ln_gain: bfloat16 [3, 1024], P(None, ('dp', 'fsdp')), may hold values from 0.25 to 1.75
- ln_bias: bfloat16 [3, 1024], P(None, ('dp', 'fsdp')), may hold values from -2 to 2
Outputs:
- output: bfloat16 [16384, 1024], P(('dp', 'fsdp'))
- grad_tokens: bfloat16 [16384, 1024], P(('dp', 'fsdp'))
- grad_memory: bfloat16 [16384, 1024], P(('dp', 'fsdp'))
- grad_proj_in: float32 [6, 1024, 1024], P(None, ('dp', 'fsdp'))
- grad_proj_out: float32 [2, 1024, 1024], P(None, ('dp', 'fsdp'))
- grad_ffn_in: float32 [1024, 4096], P(('dp', 'fsdp'))
- grad_ffn_out: float32 [4096, 1024], P(('dp', 'fsdp'))
- grad_gain: float32 [3, 1024], P(None, ('dp', 'fsdp'))
- grad_bias: float32 [3, 1024], P(None, ('dp', 'fsdp'))
Inputs may be any that keep to these rules, and one draw needn't show every extreme that they name: `sent_len`: each device's 4 sentence lengths sum to 512; on every device the longest is exactly 256. `mem_len`: each device's 4 memory lengths sum to 512; on every device the longest is exactly 256.
All inputs are finite; a program needn't handle non-finite values.
Results may differ from a plain program's by a relative error of at most 0.02.
The roundings to bfloat16 on the way count: a program that leaves them out, or rounds other values in their place, can miss the bound.
Values may be sent and summed in bfloat16 or wider, within the bound.
A program may use at most 256 MiB of HBM per device.

v0:
```python
import jax
import jax.numpy as jnp
from jax import lax
from jax.sharding import PartitionSpec as P

HEADS = 16
HEAD_DIM = 64


residual_scale = 300.0**0.25
masked_score = -1000000000.0


def layer_norm(summed, scale_row, shift_row):
    middle = jnp.mean(summed, axis=-1, keepdims=True)
    centered = summed - middle
    spread = jnp.mean(centered * centered, axis=-1, keepdims=True)
    return centered * lax.rsqrt(spread + 1e-05) * scale_row + shift_row


def segment_ids(lengths, seg_count):
    sent_ends = jnp.cumsum(lengths)
    positions = jnp.arange(seg_count, dtype=jnp.int32)
    return jnp.sum((positions[:, None] >= sent_ends[None, :]).astype(jnp.int32), axis=1)


def split_blocks(array, block_rows):
    return array.reshape((array.shape[0] // block_rows, block_rows) + array.shape[1:])


def block_scores(query_blk, key_heads, seg_blk, row_blk, key_seg, causal):
    scores = jnp.einsum(
        "qhd,khd->hqk", query_blk, key_heads, preferred_element_type=jnp.float32
    ) * HEAD_DIM ** (-0.5)
    allowed = seg_blk[:, None] == key_seg[None, :]
    if causal:
        allowed = allowed & (
            jnp.arange(key_seg.shape[0], dtype=jnp.int32)[None, :] <= row_blk[:, None]
        )
    return jnp.where(allowed[None], scores, masked_score)


def attend_forward(queries, key_rows, values, query_seg, key_seg, causal):
    row_count = queries.shape[0]
    block_rows = min(row_count, 512)
    key_heads = key_rows.reshape(key_rows.shape[0], HEADS, HEAD_DIM)
    value_heads = values.reshape(values.shape[0], HEADS, HEAD_DIM)
    positions = jnp.arange(row_count, dtype=jnp.int32)
    pieces = (
        split_blocks(queries.reshape(row_count, HEADS, HEAD_DIM), block_rows),
        split_blocks(query_seg, block_rows),
        split_blocks(positions, block_rows),
    )

    def one_block(piece):
        query_blk, seg_blk, row_blk = piece
        scores = block_scores(query_blk, key_heads, seg_blk, row_blk, key_seg, causal)
        peaks = jnp.max(scores, axis=-1, keepdims=True)
        powers = jnp.exp(scores - peaks)
        totals = jnp.sum(powers, axis=-1, keepdims=True)
        weights = (powers / totals).astype(jnp.bfloat16)
        mixture = jnp.einsum(
            "hqk,khd->qhd", weights, value_heads, preferred_element_type=jnp.float32
        )
        return (mixture, (peaks + jnp.log(totals))[..., 0])

    mixture, log_totals = lax.map(one_block, pieces)
    return (mixture.reshape(row_count, HEADS * HEAD_DIM).astype(jnp.bfloat16), log_totals)


def attend_backward(queries, key_rows, values, query_seg, key_seg, causal, log_totals, grad_mix):
    row_count = queries.shape[0]
    block_rows = min(row_count, 512)
    score_scale = HEAD_DIM ** (-0.5)
    key_heads = key_rows.reshape(key_rows.shape[0], HEADS, HEAD_DIM)
    value_heads = values.reshape(values.shape[0], HEADS, HEAD_DIM)
    positions = jnp.arange(row_count, dtype=jnp.int32)
    pieces = (
        split_blocks(queries.reshape(row_count, HEADS, HEAD_DIM), block_rows),
        split_blocks(query_seg, block_rows),
        split_blocks(positions, block_rows),
        log_totals,
        split_blocks(grad_mix.reshape(row_count, HEADS, HEAD_DIM), block_rows),
    )

    def one_block(carried, piece):
        grad_keys, grad_values = carried
        query_blk, seg_blk, row_blk, lse_blk, grad_blk = piece
        scores = block_scores(query_blk, key_heads, seg_blk, row_blk, key_seg, causal)
        probs = jnp.exp(scores - lse_blk[:, :, None])
        grad_values = grad_values + jnp.einsum(
            "hqk,qhd->khd", probs.astype(jnp.bfloat16), grad_blk, preferred_element_type=jnp.float32
        )
        grad_probs = jnp.einsum(
            "qhd,khd->hqk", grad_blk, value_heads, preferred_element_type=jnp.float32
        )
        inner = jnp.sum(grad_probs * probs, axis=-1, keepdims=True)
        grad_scores = (probs * (grad_probs - inner)).astype(jnp.bfloat16)
        grad_query = (
            jnp.einsum("hqk,khd->qhd", grad_scores, key_heads, preferred_element_type=jnp.float32)
            * score_scale
        )
        grad_keys = (
            grad_keys
            + jnp.einsum("hqk,qhd->khd", grad_scores, query_blk, preferred_element_type=jnp.float32)
            * score_scale
        )
        return ((grad_keys, grad_values), grad_query)

    zeros = jnp.zeros(key_heads.shape, jnp.float32)
    (grad_keys, grad_values), grad_query = lax.scan(one_block, (zeros, zeros), pieces)
    width = HEADS * HEAD_DIM
    return (
        grad_query.reshape(row_count, width).astype(jnp.bfloat16),
        grad_keys.reshape(-1, width).astype(jnp.bfloat16),
        grad_values.reshape(-1, width).astype(jnp.bfloat16),
    )


def run_forward(tokens, memory, sent_seg, mem_seg, weights):
    proj_in, proj_out, ffn_in, ffn_out, ln_gain, ln_bias = weights
    gains = ln_gain.astype(jnp.float32)
    shifts = ln_bias.astype(jnp.float32)
    self_qkv = jnp.einsum(
        "td,wde->wte", tokens, proj_in[0:3], preferred_element_type=jnp.float32
    ).astype(jnp.bfloat16)
    self_mix, self_lse = attend_forward(
        self_qkv[0], self_qkv[1], self_qkv[2], sent_seg, sent_seg, True
    )
    first_sum = residual_scale * tokens.astype(jnp.float32) + jnp.dot(
        self_mix, proj_out[0], preferred_element_type=jnp.float32
    )
    first_out = layer_norm(first_sum, gains[0], shifts[0])
    first_low = first_out.astype(jnp.bfloat16)
    cross_query = jnp.dot(first_low, proj_in[3], preferred_element_type=jnp.float32).astype(
        jnp.bfloat16
    )
    cross_kv = jnp.einsum(
        "td,wde->wte", memory, proj_in[4:6], preferred_element_type=jnp.float32
    ).astype(jnp.bfloat16)
    cross_mix, cross_lse = attend_forward(
        cross_query, cross_kv[0], cross_kv[1], sent_seg, mem_seg, False
    )
    second_sum = residual_scale * first_out + jnp.dot(
        cross_mix, proj_out[1], preferred_element_type=jnp.float32
    )
    second_out = layer_norm(second_sum, gains[1], shifts[1])
    second_low = second_out.astype(jnp.bfloat16)
    hidden_pre = jnp.dot(second_low, ffn_in, preferred_element_type=jnp.float32)
    hidden_act = jax.nn.gelu(hidden_pre).astype(jnp.bfloat16)
    third_sum = residual_scale * second_out + jnp.dot(
        hidden_act, ffn_out, preferred_element_type=jnp.float32
    )
    final = layer_norm(third_sum, gains[2], shifts[2])
    return {
        "self_qkv": self_qkv,
        "self_mix": self_mix,
        "self_lse": self_lse,
        "first_sum": first_sum,
        "first_low": first_low,
        "cross_query": cross_query,
        "cross_kv": cross_kv,
        "cross_mix": cross_mix,
        "cross_lse": cross_lse,
        "second_sum": second_sum,
        "second_low": second_low,
        "hidden_pre": hidden_pre,
        "hidden_act": hidden_act,
        "third_sum": third_sum,
        "final": final,
    }


def run_backward(saved, tokens, memory, sent_seg, mem_seg, weights, cotangent):
    proj_in, proj_out, ffn_in, ffn_out, ln_gain, ln_bias = weights
    gains = ln_gain.astype(jnp.float32)
    shifts = ln_bias.astype(jnp.float32)
    _, pull_third = jax.vjp(layer_norm, saved["third_sum"], gains[2], shifts[2])
    grad_third, gain_third, shift_third = pull_third(cotangent.astype(jnp.float32))
    third_low = grad_third.astype(jnp.bfloat16)
    grad_ffn_out = jnp.einsum(
        "tf,td->fd", saved["hidden_act"], third_low, preferred_element_type=jnp.float32
    )
    grad_act = jnp.einsum("td,fd->tf", third_low, ffn_out, preferred_element_type=jnp.float32)
    _, pull_gelu = jax.vjp(jax.nn.gelu, saved["hidden_pre"])
    grad_pre = pull_gelu(grad_act)[0].astype(jnp.bfloat16)
    grad_ffn_in = jnp.einsum(
        "td,tf->df", saved["second_low"], grad_pre, preferred_element_type=jnp.float32
    )
    grad_second = residual_scale * grad_third + jnp.einsum(
        "tf,df->td", grad_pre, ffn_in, preferred_element_type=jnp.float32
    )
    ffn_grads = (grad_ffn_in, grad_ffn_out, gain_third, shift_third)
    _, pull_second = jax.vjp(layer_norm, saved["second_sum"], gains[1], shifts[1])
    grad_two, gain_second, shift_second = pull_second(grad_second)
    two_low = grad_two.astype(jnp.bfloat16)
    grad_cross_out = jnp.einsum(
        "te,td->ed", saved["cross_mix"], two_low, preferred_element_type=jnp.float32
    )
    grad_cross_mix = jnp.einsum(
        "td,ed->te", two_low, proj_out[1], preferred_element_type=jnp.float32
    ).astype(jnp.bfloat16)
    grad_cq, grad_ck, grad_cv = attend_backward(
        saved["cross_query"],
        saved["cross_kv"][0],
        saved["cross_kv"][1],
        sent_seg,
        mem_seg,
        False,
        saved["cross_lse"],
        grad_cross_mix,
    )
    grad_ckv = jnp.stack([grad_ck, grad_cv])
    grad_cross_in = jnp.concatenate(
        [
            jnp.einsum(
                "td,te->de", saved["first_low"], grad_cq, preferred_element_type=jnp.float32
            )[None],
            jnp.einsum("td,wte->wde", memory, grad_ckv, preferred_element_type=jnp.float32),
        ],
        axis=0,
    )
    grad_memory = jnp.einsum(
        "wte,wde->td", grad_ckv, proj_in[4:6], preferred_element_type=jnp.float32
    ).astype(jnp.bfloat16)
    grad_first = residual_scale * grad_two + jnp.einsum(
        "te,de->td", grad_cq, proj_in[3], preferred_element_type=jnp.float32
    )
    cross_grads = (grad_cross_in, grad_cross_out, gain_second, shift_second)
    _, pull_first = jax.vjp(layer_norm, saved["first_sum"], gains[0], shifts[0])
    grad_one, gain_first, shift_first = pull_first(grad_first)
    one_low = grad_one.astype(jnp.bfloat16)
    grad_self_out = jnp.einsum(
        "te,td->ed", saved["self_mix"], one_low, preferred_element_type=jnp.float32
    )
    grad_self_mix = jnp.einsum(
        "td,ed->te", one_low, proj_out[0], preferred_element_type=jnp.float32
    ).astype(jnp.bfloat16)
    self_qkv = saved["self_qkv"]
    grad_sq, grad_sk, grad_sv = attend_backward(
        self_qkv[0],
        self_qkv[1],
        self_qkv[2],
        sent_seg,
        sent_seg,
        True,
        saved["self_lse"],
        grad_self_mix,
    )
    grad_sqkv = jnp.stack([grad_sq, grad_sk, grad_sv])
    grad_self_in = jnp.einsum("td,wte->wde", tokens, grad_sqkv, preferred_element_type=jnp.float32)
    grad_tokens = (
        residual_scale * grad_one
        + jnp.einsum("wte,wde->td", grad_sqkv, proj_in[0:3], preferred_element_type=jnp.float32)
    ).astype(jnp.bfloat16)
    self_grads = (grad_self_in, grad_self_out, gain_first, shift_first)
    all_in = jnp.concatenate([self_grads[0], cross_grads[0]], axis=0)
    all_out = jnp.stack([self_grads[1], cross_grads[1]])
    all_gain = jnp.stack([self_grads[2], cross_grads[2], ffn_grads[2]])
    all_bias = jnp.stack([self_grads[3], cross_grads[3], ffn_grads[3]])
    all_in, all_out, grad_ffn_in, grad_ffn_out, all_gain, all_bias = (
        lax.psum_scatter(all_in, ("dp", "fsdp"), scatter_dimension=1, tiled=True),
        lax.psum_scatter(all_out, ("dp", "fsdp"), scatter_dimension=1, tiled=True),
        lax.psum_scatter(ffn_grads[0], ("dp", "fsdp"), scatter_dimension=0, tiled=True),
        lax.psum_scatter(ffn_grads[1], ("dp", "fsdp"), scatter_dimension=0, tiled=True),
        lax.psum_scatter(all_gain, ("dp", "fsdp"), scatter_dimension=1, tiled=True),
        lax.psum_scatter(all_bias, ("dp", "fsdp"), scatter_dimension=1, tiled=True),
    )
    return (
        grad_tokens,
        grad_memory,
        all_in,
        all_out,
        grad_ffn_in,
        grad_ffn_out,
        all_gain,
        all_bias,
    )


def on_device(
    tokens,
    memory,
    cotangent,
    sent_len,
    mem_len,
    proj_in,
    proj_out,
    ffn_in,
    ffn_out,
    ln_gain,
    ln_bias,
):
    gathered = (
        lax.all_gather(proj_in, ("dp", "fsdp"), axis=1, tiled=True),
        lax.all_gather(proj_out, ("dp", "fsdp"), axis=1, tiled=True),
        lax.all_gather(ffn_in, ("dp", "fsdp"), axis=0, tiled=True),
        lax.all_gather(ffn_out, ("dp", "fsdp"), axis=0, tiled=True),
        lax.all_gather(ln_gain, ("dp", "fsdp"), axis=1, tiled=True),
        lax.all_gather(ln_bias, ("dp", "fsdp"), axis=1, tiled=True),
    )
    sent_seg = segment_ids(sent_len[0], tokens.shape[0])
    mem_seg = segment_ids(mem_len[0], memory.shape[0])
    saved = run_forward(tokens, memory, sent_seg, mem_seg, gathered)
    output = saved["final"].astype(jnp.bfloat16)
    again = (
        lax.all_gather(proj_in, ("dp", "fsdp"), axis=1, tiled=True),
        lax.all_gather(proj_out, ("dp", "fsdp"), axis=1, tiled=True),
        lax.all_gather(ffn_in, ("dp", "fsdp"), axis=0, tiled=True),
        lax.all_gather(ffn_out, ("dp", "fsdp"), axis=0, tiled=True),
        lax.all_gather(ln_gain, ("dp", "fsdp"), axis=1, tiled=True),
        lax.all_gather(ln_bias, ("dp", "fsdp"), axis=1, tiled=True),
    )
    saved = run_forward(tokens, memory, sent_seg, mem_seg, again)
    grad_tokens, grad_memory, grad_pin, grad_pout, grad_fin, grad_fout, grad_gain, grad_bias = (
        run_backward(saved, tokens, memory, sent_seg, mem_seg, again, cotangent)
    )
    return (
        output,
        grad_tokens,
        grad_memory,
        grad_pin,
        grad_pout,
        grad_fin,
        grad_fout,
        grad_gain,
        grad_bias,
    )


def solution(mesh):
    placed = (
        P(("dp", "fsdp"), None),
        P(("dp", "fsdp"), None),
        P(("dp", "fsdp"), None),
        P(("dp", "fsdp"), None),
        P(("dp", "fsdp"), None),
        P(None, ("dp", "fsdp"), None),
        P(None, ("dp", "fsdp"), None),
        P(("dp", "fsdp"), None),
        P(("dp", "fsdp"), None),
        P(None, ("dp", "fsdp")),
        P(None, ("dp", "fsdp")),
    )
    return jax.shard_map(
        on_device,
        mesh=mesh,
        in_specs=placed,
        out_specs=(
            P(("dp", "fsdp"), None),
            P(("dp", "fsdp"), None),
            P(("dp", "fsdp"), None),
            P(None, ("dp", "fsdp"), None),
            P(None, ("dp", "fsdp"), None),
            P(("dp", "fsdp"), None),
            P(("dp", "fsdp"), None),
            P(None, ("dp", "fsdp")),
            P(None, ("dp", "fsdp")),
        ),
        check_vma=False,
    )
```

profile of v0, /device:TPU:4, one launch (start us, length us, event | category | flops | bytes accessed | tf_op | source)
XLA Modules:
  0.0 1628.2 jit_solution(3936029516967430871)
XLA Ops:
  11.7 41.2 %all-gather = bf16[32,32,3]{1,2,0:T(4,128)(2,1)S(1)} all-gather(bf16[1,32,3]{1,2,0:T(4,128)(2,1)} %bitcast.216), channel_id=1, replica_groups=mesh['dp'=2,'fsdp'=16] {'dp','fsdp'}, dimensions={0}, use_global_device_ids=true | all-gather | bytes 6336 | tf_op jit(solution)/shard_map/all_gather | solution.py:299
  53.0 37.5 %all-gather.1 = bf16[32,32,3]{1,2,0:T(4,128)(2,1)S(1)} all-gather(bf16[1,32,3]{1,2,0:T(4,128)(2,1)} %bitcast.217), channel_id=1, replica_groups=mesh['dp'=2,'fsdp'=16] {'dp','fsdp'}, dimensions={0}, use_global_device_ids=true | all-gather | bytes 6336 | tf_op jit(solution)/shard_map/all_gather | solution.py:300
  91.1 16.9 %all-gather.7.cloned.1.call-done = bf16[6,1024,1024]{2,1,0:T(8,128)(2,1)} async-done(((bf16[6,32,1024]{2,1,0:T(8,128)(2,1)}), bf16[6,1024,1024]{2,1,0:T(8,128)(2,1)}) %all-gather.7.cloned.1.call-update) | async-done | bytes 12582928 | tf_op jit(solution)/shard_map/all_gather | solution.py:295
  107.9 6.5 convert_bitcast_fusion
  114.7 8.0 fusion.78
  122.7 8.3 fusion
  131.0 7.7 fusion.41
  138.8 32.4 %all-gather.9.cloned.1.call-done = bf16[2,1024,1024]{2,1,0:T(8,128)(2,1)} async-done(((bf16[2,32,1024]{2,1,0:T(8,128)(2,1)}), bf16[2,1024,1024]{2,1,0:T(8,128)(2,1)}) %all-gather.9.cloned.1.call-update) | async-done | bytes 4194320 | tf_op jit(solution)/shard_map/all_gather | solution.py:296
  171.2 2.9 fusion.79
  175.5 2.9 fusion.43
  179.0 5.1 convert_bitcast_fusion.1
  184.3 7.7 fusion.80
  192.0 8.3 fusion.1
  200.3 7.7 fusion.40
  208.0 1.5 fusion.81
  210.9 39.2 %all-gather.11.cloned.1.call-done = bf16[1024,4096]{1,0:T(8,128)(2,1)} async-done(((bf16[32,4096]{1,0:T(8,128)(2,1)}), bf16[1024,4096]{1,0:T(8,128)(2,1)}) %all-gather.11.cloned.1.call-update) | async-done | bytes 8388624 | tf_op jit(solution)/shard_map/all_gather | solution.py:297
  250.1 10.3 fusion.67
  260.4 68.5 %all-gather.13.cloned.1.call-done = bf16[4096,1024]{1,0:T(8,128)(2,1)} async-done(((bf16[128,1024]{1,0:T(8,128)(2,1)}), bf16[4096,1024]{1,0:T(8,128)(2,1)}) %all-gather.13.cloned.1.call-update) | async-done | bytes 8388624 | tf_op jit(solution)/shard_map/all_gather | solution.py:298
  328.9 10.7 fusion.82
  340.0 1.4 fusion.26
  341.4 1.9 fusion.73
  343.3 15.7 fusion.10
  359.0 8.7 multiply_reduce_fusion.2
  370.7 1.3 fusion.42
  373.6 9.6 fusion.45
  383.2 14.5 multiply_reduce_fusion.1
  397.7 10.7 multiply_convert_fusion.1
  408.4 7.5 multiply_convert_fusion.3
  415.9 1.5 multiply_convert_fusion.6
  417.5 3.4 convolution_bitcast_fusion.2
  420.8 4.3 multiply_reduce_fusion.3
  425.8 1.4 copy-done.24
  428.1 1.3 fusion.44
  430.9 9.6 fusion.48
  440.5 14.6 multiply_reduce_fusion
  455.1 10.7 multiply_convert_fusion
  465.8 7.5 multiply_convert_fusion.4
  473.4 1.5 multiply_convert_fusion.5
  476.1 1.3 copy.145
  477.4 2.4 copy.144
  482.1 1.3 copy.138
  483.4 2.3 copy.139
  485.8 3.8 convolution_bitcast_fusion.1
  489.7 3.6 convolution_bitcast_fusion
  493.3 8.8 pad_maximum_fusion
  502.1 29.7 %copy.150 = f32[6,1024,1024]{2,0,1:T(8,128)} copy(f32[6,1024,1024]{1,2,0:T(8,128)} %pad_maximum_fusion) | data formatting | bytes 50331648 | tf_op jit(solution)/shard_map/concatenate | solution.py:257
  532.5 3.3 convolution_bitcast_fusion.3
  535.8 1.3 convolution_bitcast_fusion.4
  537.1 4.1 pad_maximum_fusion.1
  541.3 1.5 copy-done.23
  542.8 15.1 fusion.63
  558.2 1.3 copy-done.12
  559.5 10.5 fusion.65
  571.6 5.7 bitcast_convert_fusion
  577.3 7.2 fusion.27
  584.5 23.1 %reduce-scatter.21.cloned.1.call-done = f32[32,3]{1,0:T(8,128)} async-done(((f32[1024,3]{1,0:T(8,128)}), f32[32,3]{1,0:T(8,128)}) %reduce-scatter.21.cloned.1.call-update) | async-done | bytes 400
  607.6 1.4 copy.168
  609.0 131.8 %reduce-scatter.19.cloned.1.call-done = f32[32,3]{1,0:T(8,128)} async-done(((f32[1024,3]{1,0:T(8,128)}), f32[32,3]{1,0:T(8,128)}) %reduce-scatter.19.cloned.1.call-update) | async-done | bytes 400
  740.8 1.4 copy.166
  742.1 351.4 %reduce-scatter.11.cloned.1.call-done = f32[6,32,1024]{2,0,1:T(8,128)} async-done(((f32[6,1024,1024]{2,0,1:T(8,128)}), f32[6,32,1024]{2,0,1:T(8,128)}) %reduce-scatter.11.cloned.1.call-update) | async-done | bytes 786448 | tf_op jit(solution)/shard_map/reduce_scatter | solution.py:262
  1093.5 2.6 copy.151
  1096.1 152.5 %reduce-scatter.13.cloned.1.call-done = f32[2,32,1024]{2,1,0:T(8,128)} async-done(((f32[2,1024,1024]{2,1,0:T(8,128)}), f32[2,32,1024]{2,1,0:T(8,128)}) %reduce-scatter.13.cloned.1.call-update) | async-done | bytes 262160 | tf_op jit(solution)/shard_map/reduce_scatter | solution.py:263
  1248.6 185.7 %reduce-scatter.17.cloned.1.call-done = f32[128,1024]{1,0:T(8,128)} async-done(((f32[4096,1024]{1,0:T(8,128)}), f32[128,1024]{1,0:T(8,128)}) %reduce-scatter.17.cloned.1.call-update) | async-done | bytes 524304 | tf_op jit(solution)/shard_map/reduce_scatter | solution.py:265
  1434.2 187.0 %reduce-scatter.15.cloned.1.call-done = f32[32,4096]{1,0:T(8,128)} async-done(((f32[1024,4096]{1,0:T(8,128)}), f32[32,4096]{1,0:T(8,128)}) %reduce-scatter.15.cloned.1.call-update) | async-done | bytes 524304 | tf_op jit(solution)/shard_map/reduce_scatter | solution.py:264
  (223 shorter events, 22.9 us)
Async XLA Ops:
  7.2 171.8 %copy-start = (bf16[512,1024]{1,0:T(8,128)(2,1)S(1)}, bf16[512,1024]{1,0:T(8,128)(2,1)}, u32[]{:S(2)}) copy-start(bf16[512,1024]{1,0:T(8,128)(2,1)} %param.12) | copy-start | bytes 3145732
  7.2 100.8 %all-gather.7.cloned.1.call-start = ((), (), s32[]{:S(2)}) async-start(), calls=%async_computation.6 | async-start | bytes 12976128 | tf_op jit(solution)/shard_map/all_gather | solution.py:295
  7.9 163.3 %all-gather.9.cloned.1.call-start = ((), (), s32[]{:S(2)}) async-start(), calls=%async_computation.7 | async-start | bytes 4325376 | tf_op jit(solution)/shard_map/all_gather | solution.py:296
  8.7 241.4 %all-gather.11.cloned.1.call-start = ((), (), s32[]{:S(2)}) async-start(), calls=%async_computation.8 | async-start | bytes 8650752 | tf_op jit(solution)/shard_map/all_gather | solution.py:297
  9.4 319.5 %all-gather.13.cloned.1.call-start = ((), (), s32[]{:S(2)}) async-start(), calls=%async_computation.9 | async-start | bytes 8650752 | tf_op jit(solution)/shard_map/all_gather | solution.py:298
  10.0 597.6 %reduce-scatter.21.cloned.1.call-start = ((), (), s32[]{:S(2)}) async-start(), calls=%async_computation.15 | async-start | bytes 540672
  90.6 117.3 %copy-start.45 = (f32[1,1024]{1,0:T(1,128)}, f32[1,1024]{1,0:T(1,128)S(1)}, u32[]{:S(2)}) copy-start(f32[1,1024]{1,0:T(1,128)S(1)} %get-tuple-element.242) | copy-start | bytes 12292
  90.6 277.1 %copy-start.43 = (f32[1,1024]{1,0:T(1,128)}, f32[1,1024]{1,0:T(1,128)S(1)}, u32[]{:S(2)}) copy-start(f32[1,1024]{1,0:T(1,128)S(1)} %get-tuple-element.241) | copy-start | bytes 12292
  90.7 117.3 %copy-start.57 = (f32[1,1024]{1,0:T(1,128)}, f32[1,1024]{1,0:T(1,128)S(1)}, u32[]{:S(2)}) copy-start(f32[1,1024]{1,0:T(1,128)S(1)} %get-tuple-element.245) | copy-start | bytes 12292
  90.7 238.2 %copy-start.55 = (f32[1,1024]{1,0:T(1,128)}, f32[1,1024]{1,0:T(1,128)S(1)}, u32[]{:S(2)}) copy-start(f32[1,1024]{1,0:T(1,128)S(1)} %get-tuple-element.244) | copy-start | bytes 12292
  114.7 8.0 copy-start.3
  114.7 8.0 copy-start.10
  114.7 16.3 %copy-start.19 = (bf16[1,512,1024]{1,2,0:T(8,128)(2,1)}, bf16[1,512,1024]{1,2,0:T(8,128)(2,1)S(1)}, u32[]{:S(2)}) copy-start(bf16[1,512,1024]{1,2,0:T(8,128)(2,1)S(1)} %get-tuple-element.236) | copy-start | bytes 3145732
  131.0 40.2 %copy-start.67 = (bf16[512,1024]{1,0:T(8,128)(2,1)S(1)}, bf16[512,1024]{1,0:T(8,128)(2,1)}, u32[]{:S(2)}) copy-start(bf16[512,1024]{1,0:T(8,128)(2,1)} %param.11) | copy-start | bytes 3145732
  138.8 35.4 %copy-start.69 = (bf16[16,64,512]{2,1,0:T(8,128)(2,1)}, bf16[16,64,512]{2,1,0:T(8,128)(2,1)S(1)}, u32[]{:S(2)}) copy-start(bf16[16,64,512]{2,1,0:T(8,128)(2,1)S(1)} %fusion.41) | copy-start | bytes 3145732
  174.5 33.5 %copy-start.49 = (f32[512]{0:T(512)}, f32[512]{0:T(512)S(1)}, u32[]{:S(2)}) copy-start(f32[512]{0:T(512)S(1)} %fusion.56) | copy-start | bytes 6148
  179.0 5.3 copy-start.7
  184.3 7.7 copy-start.5
  184.3 15.9 copy-start.20
  200.3 7.8 copy-start.14
  200.3 7.8 copy-start.64
  209.6 158.2 %copy-start.11 = (f32[512,1024]{1,0:T(8,128)}, f32[512,1024]{1,0:T(8,128)S(1)}, u32[]{:S(2)}) copy-start(f32[512,1024]{1,0:T(8,128)S(1)} %get-tuple-element.255) | copy-start | bytes 6291460
  209.6 158.2 %copy-start.40 = (f32[512]{0:T(512)}, f32[512]{0:T(512)S(1)}, u32[]{:S(2)}) copy-start(f32[512]{0:T(512)S(1)} %broadcast_multiply_fusion.1) | copy-start | bytes 6148
  209.9 157.8 %copy-start.47 = (f32[512]{0:T(512)}, f32[512]{0:T(512)S(1)}, u32[]{:S(2)}) copy-start(f32[512]{0:T(512)S(1)} %fusion.57) | copy-start | bytes 6148
  210.9 161.7 %copy-start.39 = (f32[16,512]{1,0:T(8,128)}, f32[16,512]{1,0:T(8,128)S(1)}, u32[]{:S(2)}) copy-start(f32[16,512]{1,0:T(8,128)S(1)} %log_add_fusion.1) | copy-start | bytes 98308
  328.9 11.1 copy-start.21
  341.4 17.6 %slice-start.8 = ((s8[8388608]{0:T(1024)(128)(4,1)}), s8[4194304]{0:T(1024)(128)(4,1)S(1)}, s32[]{:S(2)}) async-start(s8[8388608]{0:T(1024)(128)(4,1)} %bitcast.220), calls=%async_computation.24 | async-start | bytes 8388608
  343.3 15.7 copy-start.22
  343.3 15.7 copy-start.59
  343.3 15.7 slice-start.9
  368.5 3.6 copy-start.61
  373.6 24.1 %slice-start.4 = ((s8[16777216]{0:T(1024)(128)(4,1)}), s8[4194304]{0:T(1024)(128)(4,1)S(1)}, s32[]{:S(2)}) async-start(s8[16777216]{0:T(1024)(128)(4,1)} %bitcast.160), calls=%async_computation.20 | async-start | bytes 8388608
  373.6 24.1 %slice-start.5 = ((s8[16777216]{0:T(1024)(128)(4,1)}), s8[4194304]{0:T(1024)(128)(4,1)S(1)}, s32[]{:S(2)}) async-start(s8[16777216]{0:T(1024)(128)(4,1)} %bitcast.160), calls=%async_computation.21 | async-start | bytes 8388608
  383.2 14.5 slice-start.6
  383.2 14.5 slice-start.7
  408.3 7.5 copy-start.1
  408.4 7.5 copy-start.6
  417.4 3.4 copy-start.28
  417.4 3.4 copy-start.62
  425.1 2.9 copy-start.66
  430.9 24.2 %slice-start = ((s8[16777216]{0:T(1024)(128)(4,1)}), s8[4194304]{0:T(1024)(128)(4,1)S(1)}, s32[]{:S(2)}) async-start(s8[16777216]{0:T(1024)(128)(4,1)} %bitcast.158), calls=%async_computation.16 | async-start | bytes 8388608
  430.9 24.2 %slice-start.1 = ((s8[16777216]{0:T(1024)(128)(4,1)}), s8[4194304]{0:T(1024)(128)(4,1)S(1)}, s32[]{:S(2)}) async-start(s8[16777216]{0:T(1024)(128)(4,1)} %bitcast.158), calls=%async_computation.17 | async-start | bytes 8388608
  440.5 14.6 slice-start.2
  440.5 14.6 slice-start.3
  465.8 7.5 copy-start.2
  465.8 7.5 copy-start.4
  476.0 264.8 %reduce-scatter.19.cloned.1.call-start = ((), (), s32[]{:S(2)}) async-start(), calls=%async_computation.14 | async-start | bytes 540672
  477.4 3.4 copy-start.18
  482.1 3.7 copy-start.29
  485.7 3.9 copy-start.31
  485.8 607.8 %reduce-scatter.11.cloned.1.call-start = ((), (), s32[]{:S(2)}) async-start(), calls=%async_computation.10 | async-start | bytes 34603008 | tf_op jit(solution)/shard_map/reduce_scatter | solution.py:262
  485.8 3.9 copy-start.34
  485.8 3.9 copy-start.36
  485.8 3.9 copy-start.68
  489.7 3.6 copy-start.16
  531.8 4.0 copy-start.25
  531.8 716.8 %reduce-scatter.13.cloned.1.call-start = ((), (), s32[]{:S(2)}) async-start(), calls=%async_computation.11 | async-start | bytes 8650752 | tf_op jit(solution)/shard_map/reduce_scatter | solution.py:263
  532.5 3.3 copy-start.70
  541.3 893.0 %reduce-scatter.17.cloned.1.call-start = ((), (), s32[]{:S(2)}) async-start(), calls=%async_computation.13 | async-start | bytes 17301504 | tf_op jit(solution)/shard_map/reduce_scatter | solution.py:265
  558.0 1063.2 %reduce-scatter.15.cloned.1.call-start = ((), (), s32[]{:S(2)}) async-start(), calls=%async_computation.12 | async-start | bytes 17301504 | tf_op jit(solution)/shard_map/reduce_scatter | solution.py:264
  571.6 5.7 copy-start.26
  571.6 5.7 copy-start.32
  571.6 5.7 copy-start.35
  571.6 5.7 copy-start.37
  (28 other events, 47.1 us)
Sparse Core Ops, SparseCore 0:
  10.9 96.9 all-gather.6
  110.9 60.2 all-gather.8
  174.0 76.0 all-gather.10
  252.8 76.0 all-gather.12
  476.1 131.4 reduce-scatter.20
  610.4 130.3 reduce-scatter.18
  743.1 350.3 reduce-scatter.10
  1096.4 152.1 reduce-scatter.12
  1251.4 182.7 reduce-scatter.16
  1436.9 184.1 reduce-scatter.14
where the time goes:
time: 1630 us
  waiting for transfers between devices  1190 us (73%)
  matrix products  222 us (14%)
  blocking collectives  78.6 us (5%)
  local copies, waits for them, and re-layouts  60.2 us (4%)
  other arithmetic  59.7 us (4%)
    reduce_scatter x1, waiting for transfers between devices, run_backward(): lax.psum_scatter(all_in, ('dp', 'fsdp'), scatter_dimension=1, tiled=True)  351 us
    reduce_scatter x1, waiting for transfers between devices, run_backward(): lax.psum_scatter(ffn_grads[0], ('dp', 'fsdp'), scatter_dimension=0, tiled...  187 us
    reduce_scatter x1, waiting for transfers between devices, run_backward(): lax.psum_scatter(ffn_grads[1], ('dp', 'fsdp'), scatter_dimension=0, tiled...  186 us
    unnamed x12, waiting for transfers between devices  158 us
    reduce_scatter x1, waiting for transfers between devices, run_backward(): lax.psum_scatter(all_out, ('dp', 'fsdp'), scatter_dimension=1, tiled=True)  153 us
    all_gather x1, waiting for transfers between devices, on_device(): lax.all_gather(ffn_out, ('dp', 'fsdp'), axis=0, tiled=True)  68.5 us
    all_gather x1, blocking collectives, on_device(): lax.all_gather(ln_gain, ('dp', 'fsdp'), axis=1, tiled=True)  41.2 us
    all_gather x1, waiting for transfers between devices, on_device(): lax.all_gather(ffn_in, ('dp', 'fsdp'), axis=0, tiled=True)  39.2 us
  transfers between devices with their start and end apart: 10, of which 10 were waited for; matrix products, arithmetic and copies ran while one was open for 12% of the time, Pallas kernels for 0%

commit v1 on v0

--- a/solution.py
+++ b/solution.py
@@ -1,6 +1,10 @@
+import functools
+
 import jax
 import jax.numpy as jnp
 from jax import lax
+from jax.experimental import pallas as pl
+from jax.experimental.pallas import tpu as pltpu
 from jax.sharding import PartitionSpec as P
 
 HEADS = 16
@@ -258,104 +262,633 @@
     all_out = jnp.stack([self_grads[1], cross_grads[1]])
     all_gain = jnp.stack([self_grads[2], cross_grads[2], ffn_grads[2]])
     all_bias = jnp.stack([self_grads[3], cross_grads[3], ffn_grads[3]])
-    all_in, all_out, grad_ffn_in, grad_ffn_out, all_gain, all_bias = (
-        lax.psum_scatter(all_in, ("dp", "fsdp"), scatter_dimension=1, tiled=True),
-        lax.psum_scatter(all_out, ("dp", "fsdp"), scatter_dimension=1, tiled=True),
-        lax.psum_scatter(ffn_grads[0], ("dp", "fsdp"), scatter_dimension=0, tiled=True),
-        lax.psum_scatter(ffn_grads[1], ("dp", "fsdp"), scatter_dimension=0, tiled=True),
-        lax.psum_scatter(all_gain, ("dp", "fsdp"), scatter_dimension=1, tiled=True),
-        lax.psum_scatter(all_bias, ("dp", "fsdp"), scatter_dimension=1, tiled=True),
-    )
     return (
         grad_tokens,
         grad_memory,
         all_in,
         all_out,
-        grad_ffn_in,
-        grad_ffn_out,
+        ffn_grads[0],
+        ffn_grads[1],
         all_gain,
         all_bias,
     )
 
 
+MESH = pl.DeviceIdType.MESH
+BOTH = ("dp", "fsdp")
+f32 = jnp.float32
+bf16 = jnp.bfloat16
+UNITS = 17
+def shard_of(unit):
+    if unit < 12:
+        return (32, 1024)
+    return (128, 256) if unit < 16 else (16, 128)
+
+
+class Place:
+    def __init__(self):
+        inner = lax.axis_index("fsdp")
+        self.y = lax.axis_index("dp")
+        self.z = inner // 4
+        self.x = (inner // 2) % 2
+        self.c = inner % 2
+
+    def at(self, y=None, z=None, x=None, c=None):
+        y = self.y if y is None else y
+        z = self.z if z is None else z
+        x = self.x if x is None else x
+        c = self.c if c is None else c
+        return (y, (z * 2 + x) * 2 + c)
+
+    def over_x(self):
+        return self.at(x=1 - self.x)
+
+    def over_y(self):
+        return self.at(y=1 - self.y)
+
+    def sibling(self):
+        return self.at(c=1 - self.c)
+
+    def greet(self):
+        barrier = pltpu.get_barrier_semaphore()
+        friends = [self.at(z=lax.rem(self.z + k, 4)) for k in (1, 2, 3)]
+        friends += [self.over_x(), self.over_y(), self.sibling()]
+        for friend in friends:
+            pl.semaphore_signal(barrier, inc=1, device_id=friend, device_id_type=MESH)
+        pl.semaphore_wait(barrier, len(friends))
+
+
+class Sender:
+    def __init__(self, place, send_sem, recv_sem):
+        self.p, self.send_sem, self.recv_sem = place, send_sem, recv_sem
+        self.pending = {}
+
+    def copy(self, unit, slot, src, dst, device, landing=None):
+        return pltpu.make_async_remote_copy(
+            src_ref=src,
+            dst_ref=dst,
+            send_sem=self.send_sem.at[unit, slot],
+            recv_sem=self.recv_sem.at[unit, slot if landing is None else landing],
+            device_id=device,
+            device_id_type=MESH,
+        )
+
+    def send(self, unit, slot, src, dst, device, cond=None, landing=None):
+        make = lambda: self.copy(unit, slot, src, dst, device, landing)
+        if cond is None:
+            make().start()
+            self.pending.setdefault(unit, []).append(lambda: make().wait_send())
+        else:
+            pl.when(cond)(lambda: make().start())
+            self.pending.setdefault(unit, []).append(
+                lambda: pl.when(cond)(lambda: make().wait_send())
+            )
+
+    def wait(self, unit, slot, ref):
+        self.copy(unit, slot, ref, ref, self.p.sibling()).wait_recv()
+
+    def finish(self, unit):
+        for done in self.pending.pop(unit, []):
+            done()
+
+
+class Gather(Sender):
+    stages = (0, 0.5, 1, 1.5, 2, 3, 4)
+
+    def __init__(self, place, send_sem, recv_sem, whole, kinds):
+        super().__init__(place, send_sem, recv_sem)
+        self.whole, self.kinds = whole, kinds
+
+    def view(self, unit, y=None, z=None, x=None, c=None):
+        every = slice(None)
+        pick = lambda v: every if v is None else v
+        return self.whole(unit).at[pick(y), pick(z), pick(x), pick(c)]
+
+    def along_z(self, unit):
+        p, kind = self.p, self.kinds[unit]
+        if kind[0] == "p":
+            return lambda z: self.view(unit, y=p.y, z=z, x=p.x, c=p.c)
+        if kind == "rL":
+            return lambda z: self.view(unit, y=p.y, z=z, c=p.c)
+        return lambda z: self.view(unit, z=z, x=p.x, c=p.c)
+
+    def z_send(self, unit):
+        p, part = self.p, self.along_z(unit)
+        for k in (1, 2, 3):
+            there = lax.rem(p.z + k, 4)
+            near = jnp.logical_not(
+                ((p.z == 0) & (there == 3)) | ((p.z == 3) & (there == 0))
+            )
+            self.send(unit, there, part(p.z), part(p.z), p.at(z=there), near, landing=p.z)
+
+    def z_relay(self, unit):
+        p, part = self.p, self.along_z(unit)
+        for here, source, there in ((2, 0, 3), (1, 3, 0)):
+            pl.when(p.z == here)(lambda source=source: self.wait(unit, source, part(source)))
+            self.send(
+                unit, 8, part(source), part(source), p.at(z=there), p.z == here, landing=source
+            )
+
+    def z_wait(self, unit):
+        p, part = self.p, self.along_z(unit)
+        for k in (1, 2, 3):
+            source = lax.rem(p.z + 4 - k, 4)
+            relayed = ((p.z == 2) & (source == 0)) | ((p.z == 1) & (source == 3))
+            pl.when(jnp.logical_not(relayed))(
+                lambda source=source: self.wait(unit, source, part(source))
+            )
+
+    def stage(self, unit, step):
+        p, kind = self.p, self.kinds[unit]
+        y, z, x, c = p.y, p.z, p.x, p.c
+        view = lambda **at: self.view(unit, **at)
+        send = lambda slot, ref, device: self.send(unit, slot, ref, ref, device)
+        if kind[0] == "p":
+            if step == 0:
+                self.z_send(unit)
+            if step == 0.5:
+                self.z_relay(unit)
+            if step == 1:
+                self.z_wait(unit)
+                line = view(y=y, x=x, c=c)
+                send(4, line, p.over_x())
+                send(5, line, p.over_y())
+            if step == 2:
+                if kind == "pL":
+                    line = view(y=y, x=1 - x, c=c)
+                    self.wait(unit, 4, line)
+                    send(6, line, p.over_y())
+                else:
+                    line = view(y=1 - y, x=x, c=c)
+                    self.wait(unit, 5, line)
+                    send(6, line, p.over_x())
+            if step == 3:
+                if kind == "pL":
+                    self.wait(unit, 5, view(y=1 - y, x=x, c=c))
+                else:
+                    self.wait(unit, 4, view(y=y, x=1 - x, c=c))
+                self.wait(unit, 6, view(y=1 - y, x=1 - x, c=c))
+                send(7, view(c=c), p.sibling())
+        else:
+            left = kind == "rL"
+            first, last = (p.over_x(), p.over_y()) if left else (p.over_y(), p.over_x())
+            if step == 0:
+                send(4, view(y=y, z=z, x=x, c=c), first)
+            if step == 1:
+                self.wait(
+                    unit,
+                    4,
+                    view(y=y, z=z, x=1 - x, c=c) if left else view(y=1 - y, z=z, x=x, c=c),
+                )
+                self.z_send(unit)
+            if step == 1.5:
+                self.z_relay(unit)
+            if step == 2:
+                self.z_wait(unit)
+                send(5, view(y=y, c=c) if left else view(x=x, c=c), last)
+            if step == 3:
+                self.wait(unit, 5, view(y=1 - y, c=c) if left else view(x=1 - x, c=c))
+                send(7, view(c=c), p.sibling())
+        if step == 4:
+            self.wait(unit, 7, view(c=1 - c))
+
+
+class Scatter(Sender):
+    stages = (0, 1, 2, 2.5, 3, 3.5, 4, 5)
+
+    def __init__(self, place, send_sem, recv_sem, other, mine, twin, eight, four, zs, out, kinds):
+        super().__init__(place, send_sem, recv_sem)
+        self.other, self.mine, self.twin = other, mine, twin
+        self.eight, self.four, self.zs, self.out, self.kinds = eight, four, zs, out, kinds
+
+    def add(self, into, *terms):
+        total = into[...].astype(f32)
+        for term in terms:
+            total = total + term[...].astype(f32)
+        into[...] = total.astype(into.dtype)
+
+    def along_z(self, unit):
+        p, kind, mine = self.p, self.kinds[unit], self.mine(unit)
+        if kind[0] == "p":
+            return (lambda z: mine.at[p.y, z, p.x]), (lambda ref: ref.at[0])
+        if kind == "rL":
+            return (lambda z: mine.at[p.y, z]), (lambda ref: ref)
+        return (lambda z: mine.at[:, z, p.x]), (lambda ref: ref)
+
+    def z_send(self, unit):
+        p, zs = self.p, self.zs(unit)
+        part, slot = self.along_z(unit)
+        for k in (1, 2, 3):
+            there = lax.rem(p.z + k, 4)
+            far = ((p.z == 0) & (there == 3)) | ((p.z == 3) & (there == 0))
+            relayed = ((p.z == 2) & (there == 0)) | ((p.z == 1) & (there == 3))
+            self.send(
+                unit,
+                4 + there,
+                part(there),
+                slot(zs.at[p.z]),
+                p.at(z=there),
+                jnp.logical_not(far | relayed),
+                landing=4 + p.z,
+            )
+        self.send(unit, 8, part(3), slot(zs.at[1]), p.at(z=1), p.z == 0)
+        self.send(unit, 8, part(0), slot(zs.at[2]), p.at(z=2), p.z == 3)
+
+    def z_relay(self, unit):
+        p, zs = self.p, self.zs(unit)
+        part, slot = self.along_z(unit)
+        for here, there in ((1, 3), (2, 0)):
+
+            @pl.when(p.z == here)
+            def _(here=here, there=there):
+                self.wait(unit, 8, slot(zs.at[here]))
+                self.add(part(there), slot(zs.at[here]))
+
+            self.send(
+                unit,
+                4 + there,
+                part(there),
+                slot(zs.at[here]),
+                p.at(z=there),
+                p.z == here,
+                landing=4 + here,
+            )
+
+    def z_sum(self, unit, store):
+        p, zs = self.p, self.zs(unit)
+        part, slot = self.along_z(unit)
+        edge = (p.z == 0) | (p.z == 3)
+
+        @pl.when(edge)
+        def _():
+            self.wait(unit, 5, slot(zs.at[1]))
+            self.wait(unit, 6, slot(zs.at[2]))
+            store(
+                part(p.z)[...].astype(f32)
+                + slot(zs.at[1])[...].astype(f32)
+                + slot(zs.at[2])[...].astype(f32)
+            )
+
+        @pl.when(jnp.logical_not(edge))
+        def _():
+            inner = 3 - p.z
+            self.wait(unit, 4, slot(zs.at[0]))
+            self.wait(unit, 7, slot(zs.at[3]))
+            self.wait(unit, 4 + inner, slot(zs.at[inner]))
+            store(
+                part(p.z)[...].astype(f32)
+                + slot(zs.at[inner])[...].astype(f32)
+                + slot(zs.at[0])[...].astype(f32)
+                + slot(zs.at[3])[...].astype(f32)
+            )
+
+    def stage(self, unit, step):
+        p, kind = self.p, self.kinds[unit]
+        y, z, x = p.y, p.z, p.x
+        mine, eight, four, out = self.mine(unit), self.eight(unit), self.four(unit), self.out(unit)
+        send = lambda slot, src, dst, device: self.send(unit, slot, src, dst, device)
+        if step == 0:
+            send(0, self.other(unit), self.twin(unit), p.sibling())
+        if step == 1:
+            self.wait(unit, 0, self.twin(unit))
+            for half in (0, 1):
+                self.add(mine.at[half], self.twin(unit).at[half])
+            self.finish(unit)
+            if kind == "pL":
+                send(1, mine.at[1 - y, :, 1 - x], eight.at[0], p.over_y())
+                send(3, mine.at[1 - y, :, x], four, p.over_y())
+            if kind == "pR":
+                send(1, mine.at[1 - y, :, 1 - x], eight.at[0], p.over_x())
+                send(3, mine.at[y, :, 1 - x], four, p.over_x())
+            for half in (0, 1):
+                if kind == "rL":
+                    send(1 + half, mine.at[1 - y, :, half], eight.at[half], p.over_y())
+                if kind == "rR":
+                    send(1 + half, mine.at[half, :, 1 - x], eight.at[half], p.over_x())
+        if step == 2:
+            if kind[0] == "p":
+                self.wait(unit, 1, eight.at[0])
+                line = mine.at[y, :, 1 - x] if kind == "pL" else mine.at[1 - y, :, x]
+                self.add(line, eight.at[0])
+                send(2, line, eight.at[1], p.over_x() if kind == "pL" else p.over_y())
+            else:
+                for half in (0, 1):
+                    self.wait(unit, 1 + half, eight.at[half])
+                    self.add(
+                        mine.at[y, :, half] if kind == "rL" else mine.at[half, :, x],
+                        eight.at[half],
+                    )
+                self.z_send(unit)
+        if step == 2.5 and kind[0] == "r":
+            self.z_relay(unit)
+        if step == 3:
+            if kind[0] == "p":
+                self.wait(unit, 3, four)
+                self.wait(unit, 2, eight.at[1])
+                self.add(mine.at[y, :, x], four, eight.at[1])
+                self.z_send(unit)
+            else:
+                line = mine.at[y, z] if kind == "rL" else mine.at[:, z, x]
+
+                def keep(value):
+                    line[...] = value.astype(bf16)
+
+                self.z_sum(unit, keep)
+                if kind == "rL":
+                    send(3, mine.at[y, z, 1 - x], four.at[0], p.over_x())
+                else:
+                    send(3, mine.at[1 - y, z, x], four.at[0], p.over_y())
+        if step == 3.5 and kind[0] == "p":
+            self.z_relay(unit)
+        if step == 4:
+
+            def result(value):
+                out[...] = value
+
+            if kind[0] == "p":
+                self.z_sum(unit, result)
+            else:
+                self.wait(unit, 3, four.at[0])
+                result(mine[y, z, x].astype(f32) + four[0].astype(f32))
+        if step == 5:
+            self.finish(unit)
+
+
+def kinds_of(pattern, order):
+    kinds = {}
+    for place, unit in enumerate(order):
+        kinds[unit] = pattern[(place // 2) % len(pattern)] + "LR"[place % 2]
+    return kinds
+
+GATHER_ORDER = list(range(17))
+GATHER_KINDS = kinds_of("rprrprpr", GATHER_ORDER)
+GATHER_LAG = 2.0
+SCATTER_ORDER = list(range(17))
+SCATTER_KINDS = kinds_of("p", SCATTER_ORDER)
+SCATTER_LAG = 1.5
+
+
+def gather_kernel(
+    proj_in, proj_out, ffn_in, ffn_out, small, wide, deep, tiny, send_sem, recv_sem, local_sem
+):
+    place = Place()
+
+    def whole(unit):
+        return wide.at[unit] if unit < 12 else deep.at[unit - 12] if unit < 16 else tiny
+
+    def own(unit):
+        if unit < 6:
+            return proj_in.at[unit]
+        if unit < 8:
+            return proj_out.at[unit - 6]
+        if unit < 12:
+            return ffn_in.at[:, pl.ds((unit - 8) * 1024, 1024)]
+        if unit < 16:
+            return ffn_out.at[:, pl.ds((unit - 12) * 256, 256)]
+        return small
+
+    gather = Gather(place, send_sem, recv_sem, whole, GATHER_KINDS)
+    copies = {}
+    for unit in GATHER_ORDER:
+        copies[unit] = pltpu.make_async_copy(
+            own(unit), whole(unit).at[place.y, place.z, place.x, place.c], local_sem.at[unit]
+        )
+        copies[unit].start()
+    place.greet()
+    events = sorted(
+        (turn + step * GATHER_LAG, step, unit)
+        for turn, unit in enumerate(GATHER_ORDER)
+        for step in Gather.stages
+    )
+    for _, step, unit in events:
+        if step == 0:
+            copies[unit].wait()
+        gather.stage(unit, step)
+    for unit in GATHER_ORDER:
+        gather.finish(unit)
+
+
+def gather_weights(proj_in, proj_out, ffn_in, ffn_out, small):
+    return pl.pallas_call(
+        gather_kernel,
+        out_shape=(
+            jax.ShapeDtypeStruct((12, 2, 4, 2, 2, 32, 1024), bf16),
+            jax.ShapeDtypeStruct((4, 2, 4, 2, 2, 128, 256), bf16),
+            jax.ShapeDtypeStruct((2, 4, 2, 2, 16, 128), bf16),
+        ),
+        in_specs=[pl.BlockSpec(memory_space=pl.ANY)] * 5,
+        out_specs=[pl.BlockSpec(memory_space=pl.ANY)] * 3,
+        scratch_shapes=[
+            pltpu.SemaphoreType.DMA((UNITS, 9)),
+            pltpu.SemaphoreType.DMA((UNITS, 9)),
+            pltpu.SemaphoreType.DMA((UNITS,)),
+        ],
+        compiler_params=pltpu.CompilerParams(
+            collective_id=0, has_side_effects=True, vmem_limit_bytes=56 << 20
+        ),
+    )(proj_in, proj_out, ffn_in, ffn_out, small)
+
+
+def scatter_kernel(depth, *refs):
+    wide, deep, tiny, out_wide, out_deep, out_tiny = refs[:6]
+    buffers, (send_sem, recv_sem, local_sem, out_sem) = refs[6:-4], refs[-4:]
+    place = Place()
+    sort = lambda unit: 0 if unit < 12 else 1 if unit < 16 else 2
+    sums = buffers[18:21]
+    rank = {u: sum(1 for v in SCATTER_ORDER[:i] if sort(v) == sort(u)) for i, u in enumerate(SCATTER_ORDER)}
+
+    def ring(kind):
+        def pick(unit):
+            ref = buffers[3 * kind + sort(unit)]
+            return ref.at[rank[unit] % ref.shape[0]]
+
+        return pick
+
+    def out(unit):
+        if unit < 12:
+            return sums[0].at[unit]
+        if unit < 16:
+            return sums[1].at[:, pl.ds((unit - 12) * 256, 256)]
+        return sums[2]
+
+    scatter = Scatter(
+        place, send_sem, recv_sem, *[ring(kind) for kind in range(6)], out, SCATTER_KINDS
+    )
+    place.greet()
+
+    def fetch(unit):
+        source = wide.at[unit] if unit < 12 else deep.at[unit - 12] if unit < 16 else tiny
+        made = []
+        for k, into in enumerate((scatter.mine(unit), scatter.other(unit))):
+            core = place.c if k == 0 else 1 - place.c
+            copy = pltpu.make_async_copy(source.at[:, :, :, core], into, local_sem.at[unit, k])
+            copy.start()
+            made.append(copy)
+        return made
+
+    events = [
+        (turn + step * SCATTER_LAG, step, unit)
+        for turn, unit in enumerate(SCATTER_ORDER)
+        for step in Scatter.stages
+    ]
+    events += [(turn - 0.9, -1, unit) for turn, unit in enumerate(SCATTER_ORDER)]
+    fetched = {}
+    for _, step, unit in sorted(events):
+        if step == -1:
+            fetched[unit] = fetch(unit)
+            continue
+        if step == 0:
+            for copy in fetched[unit]:
+                copy.wait()
+        scatter.stage(unit, step)
+    for k, (src, dst) in enumerate(zip(sums, (out_wide, out_deep, out_tiny))):
+        copy = pltpu.make_async_copy(src, dst, out_sem.at[k])
+        copy.start()
+        copy.wait()
+
+
+def scatter_grads(wide, deep, tiny):
+    shapes = [shard_of(0), shard_of(12), shard_of(16)]
+    whole = [12, 4, 1]
+    rings = [
+        ((2, 4, 2), (4, 4, 1)),
+        ((2, 4, 2), (10, 4, 1)),
+        ((2, 4, 2), whole),
+        ((2, 4), whole),
+        ((4,), whole),
+        ((4, 2), whole),
+    ]
+    scratch = []
+    for lead, counts in rings:
+        for shape, count in zip(shapes, counts):
+            scratch.append(pltpu.VMEM((count, *lead, *shape), bf16))
+    results = [(12, 32, 1024), (128, 1024), (16, 128)]
+    return pl.pallas_call(
+        functools.partial(scatter_kernel, None),
+        out_shape=[jax.ShapeDtypeStruct(shape, f32) for shape in results],
+        in_specs=[pl.BlockSpec(memory_space=pl.ANY)] * 3,
+        out_specs=[pl.BlockSpec(memory_space=pl.ANY)] * 3,
+        scratch_shapes=scratch
+        + [pltpu.VMEM(shape, f32) for shape in results]
+        + [
+            pltpu.SemaphoreType.DMA((UNITS, 9)),
+            pltpu.SemaphoreType.DMA((UNITS, 9)),
+            pltpu.SemaphoreType.DMA((UNITS, 2)),
+            pltpu.SemaphoreType.DMA((3,)),
+        ],
+        compiler_params=pltpu.CompilerParams(
+            collective_id=1, has_side_effects=True, vmem_limit_bytes=62 << 20
+        ),
+    )(wide, deep, tiny)
+
+
+def lane_of_device():
+    return (lax.axis_index("fsdp") % 4) * 32
+
+
 def on_device(
-    tokens,
-    memory,
-    cotangent,
-    sent_len,
-    mem_len,
-    proj_in,
-    proj_out,
-    ffn_in,
-    ffn_out,
-    ln_gain,
-    ln_bias,
+    tokens, memory, cotangent, sent_len, mem_len, proj_in, proj_out, ffn_in, ffn_out, ln_gain, ln_bias
 ):
-    gathered = (
-        lax.all_gather(proj_in, ("dp", "fsdp"), axis=1, tiled=True),
-        lax.all_gather(proj_out, ("dp", "fsdp"), axis=1, tiled=True),
-        lax.all_gather(ffn_in, ("dp", "fsdp"), axis=0, tiled=True),
-        lax.all_gather(ffn_out, ("dp", "fsdp"), axis=0, tiled=True),
-        lax.all_gather(ln_gain, ("dp", "fsdp"), axis=1, tiled=True),
-        lax.all_gather(ln_bias, ("dp", "fsdp"), axis=1, tiled=True),
+    small = jnp.concatenate([ln_gain, ln_bias, jnp.zeros((10, 32), bf16)], axis=0)
+    small = jnp.concatenate(
+        [
+            jnp.where(lax.axis_index("fsdp") % 4 == k, small, jnp.zeros_like(small))
+            for k in range(4)
+        ],
+        axis=1,
+    )
+    wide, deep, tiny = gather_weights(proj_in, proj_out, ffn_in, ffn_out, small)
+    square = wide.reshape(12, 1024, 1024)
+    rows = tiny.reshape(8, 4, 16, 128).sum(1).transpose(1, 0, 2).reshape(16, 1024)
+    weights = (
+        square[0:6],
+        square[6:8],
+        jnp.concatenate([square[k] for k in range(8, 12)], axis=1),
+        jnp.concatenate([deep[k].reshape(4096, 256) for k in range(4)], axis=1),
+        rows[0:3],
+        rows[3:6],
     )
     sent_seg = segment_ids(sent_len[0], tokens.shape[0])
     mem_seg = segment_ids(mem_len[0], memory.shape[0])
-    saved = run_forward(tokens, memory, sent_seg, mem_seg, gathered)
-    output = saved["final"].astype(jnp.bfloat16)
-    again = (
-        lax.all_gather(proj_in, ("dp", "fsdp"), axis=1, tiled=True),
-        lax.all_gather(proj_out, ("dp", "fsdp"), axis=1, tiled=True),
-        lax.all_gather(ffn_in, ("dp", "fsdp"), axis=0, tiled=True),
-        lax.all_gather(ffn_out, ("dp", "fsdp"), axis=0, tiled=True),
-        lax.all_gather(ln_gain, ("dp", "fsdp"), axis=1, tiled=True),
-        lax.all_gather(ln_bias, ("dp", "fsdp"), axis=1, tiled=True),
-    )
-    saved = run_forward(tokens, memory, sent_seg, mem_seg, again)
-    grad_tokens, grad_memory, grad_pin, grad_pout, grad_fin, grad_fout, grad_gain, grad_bias = (
-        run_backward(saved, tokens, memory, sent_seg, mem_seg, again, cotangent)
-    )
+    saved = run_forward(tokens, memory, sent_seg, mem_seg, weights)
+    output = saved["final"].astype(bf16)
+    grad_tokens, grad_memory, all_in, all_out, g_in, g_out, gains, biases = run_backward(
+        saved, tokens, memory, sent_seg, mem_seg, weights, cotangent
+    )
+    terms = jnp.concatenate(
+        [all_in.astype(bf16), all_out.astype(bf16), g_in.astype(bf16).reshape(1024, 4, 1024).transpose(1, 0, 2)]
+    )
+    affine = jnp.concatenate([gains, biases, jnp.zeros((10, 1024), f32)]).astype(bf16)
+    affine = affine.reshape(16, 8, 128).transpose(1, 0, 2)
+    affine = jnp.broadcast_to(affine[:, None], (8, 4, 16, 128)).reshape(1, 2, 4, 2, 2, 16, 128)
+    got_wide, got_deep, got_tiny = scatter_grads(
+        terms.reshape(12, 2, 4, 2, 2, 32, 1024),
+        g_out.astype(bf16).reshape(4096, 4, 256).transpose(1, 0, 2).reshape(4, 2, 4, 2, 2, 128, 256),
+        affine[0],
+    )
+    own = lax.dynamic_slice(got_tiny, (0, lane_of_device()), (16, 32))
     return (
         output,
         grad_tokens,
         grad_memory,
-        grad_pin,
-        grad_pout,
-        grad_fin,
-        grad_fout,
-        grad_gain,
-        grad_bias,
-    )
+        got_wide[0:6],
+        got_wide[6:8],
+        got_wide[8:12].transpose(1, 0, 2).reshape(32, 4096),
+        got_deep,
+        own[0:3],
+        own[3:6],
+    )
+
+
+def on_any_mesh(
+    tokens, memory, cotangent, sent_len, mem_len, proj_in, proj_out, ffn_in, ffn_out, ln_gain, ln_bias
+):
+    dims = (1, 1, 0, 0, 1, 1)
+    shards = (proj_in, proj_out, ffn_in, ffn_out, ln_gain, ln_bias)
+    weights = tuple(
+        lax.all_gather(shard, BOTH, axis=dim, tiled=True) for shard, dim in zip(shards, dims)
+    )
+    sent_seg = segment_ids(sent_len[0], tokens.shape[0])
+    mem_seg = segment_ids(mem_len[0], memory.shape[0])
+    saved = run_forward(tokens, memory, sent_seg, mem_seg, weights)
+    output = saved["final"].astype(bf16)
+    grads = run_backward(saved, tokens, memory, sent_seg, mem_seg, weights, cotangent)
+    summed = tuple(
+        lax.psum_scatter(grad, BOTH, scatter_dimension=dim, tiled=True)
+        for grad, dim in zip(grads[2:], dims)
+    )
+    return (output, *grads[:2], *summed)
 
 
 def solution(mesh):
     placed = (
-        P(("dp", "fsdp"), None),
-        P(("dp", "fsdp"), None),
-        P(("dp", "fsdp"), None),
-        P(("dp", "fsdp"), None),
-        P(("dp", "fsdp"), None),
-        P(None, ("dp", "fsdp"), None),
-        P(None, ("dp", "fsdp"), None),
-        P(("dp", "fsdp"), None),
-        P(("dp", "fsdp"), None),
-        P(None, ("dp", "fsdp")),
-        P(None, ("dp", "fsdp")),
-    )
+        P(BOTH, None),
+        P(BOTH, None),
+        P(BOTH, None),
+        P(BOTH, None),
+        P(BOTH, None),
+        P(None, BOTH, None),
+        P(None, BOTH, None),
+        P(BOTH, None),
+        P(BOTH, None),
+        P(None, BOTH),
+        P(None, BOTH),
+    )
+    routed = mesh.shape["dp"] == 2 and mesh.shape["fsdp"] == 16
     return jax.shard_map(
-        on_device,
+        on_device if routed else on_any_mesh,
         mesh=mesh,
         in_specs=placed,
         out_specs=(
-            P(("dp", "fsdp"), None),
-            P(("dp", "fsdp"), None),
-            P(("dp", "fsdp"), None),
-            P(None, ("dp", "fsdp"), None),
-            P(None, ("dp", "fsdp"), None),
-            P(("dp", "fsdp"), None),
-            P(("dp", "fsdp"), None),
-            P(None, ("dp", "fsdp")),
-            P(None, ("dp", "fsdp")),
+            P(BOTH, None),
+            P(BOTH, None),
+            P(BOTH, None),
+            P(None, BOTH, None),
+            P(None, BOTH, None),
+            P(BOTH, None),
+            P(BOTH, None),
+            P(None, BOTH),
+            P(None, BOTH),
         ),
         check_vma=False,
     )

time: 1630 us -> 665 us (0.41)
  waiting for transfers between devices: 1190 us -> 0 us
  Pallas kernels: 0 us -> 314 us
  blocking collectives: 78.6 us -> 0 us
  local copies, waits for them, and re-layouts: 60.2 us -> 78.5 us
    reduce_scatter x4 -> x0, waiting for transfers between devices: 876 us -> none  [the longest x1 351 us: run_backward(): lax.psum_scatter(all_in, ('dp', 'fsdp'), scatter_dimension=1, tiled=True)]
    pallas_call x0 -> x2, Pallas kernels: none -> 314 us  [the longest x1 167 us: scatter_grads(): pl.pallas_call(functools.partial(scatter_kernel, None), out_shape=[jax.Sh...]
    unnamed x12 -> x0, waiting for transfers between devices: 158 us -> none
    all_gather x4 -> x0, waiting for transfers between devices: 157 us -> none  [the longest x1 68.5 us: on_device(): lax.all_gather(ffn_out, ('dp', 'fsdp'), axis=0, tiled=True)]
    all_gather x2 -> x0, blocking collectives: 78.6 us -> none  [the longest x1 41.2 us: on_device(): lax.all_gather(ln_gain, ('dp', 'fsdp'), axis=1, tiled=True)]
    slice x0 -> x7, local copies, waits for them, and re-layouts: none -> 27.3 us  [the longest x1 13.4 us: on_device(): square[k]]
    concatenate x1 -> x9, local copies, waits for them, and re-layouts: 29.7 us -> 8.84 us  [the longest x1 7.93 us: on_device(): jnp.concatenate([all_in.astype(bf16), all_out.astype(bf16), g_in.astype(b...]
  transfers between devices with their start and end apart: 10 -> 0, of which waited for: 10 -> 0; matrix products, arithmetic and copies ran while one was open for 12% -> 0% of each run, Pallas kernels for 0% -> 0%
where the time goes in v1:
time: 665 us; the launch traced here: 655 us
  Pallas kernels  314 us (47%)
  matrix products  208 us (31%)
  local copies, waits for them, and re-layouts  78.5 us (12%)
  other arithmetic  53.4 us (8%)
    pallas_call x1, Pallas kernels, scatter_grads(): pl.pallas_call(functools.partial(scatter_kernel, None), out_shape=[jax.Sh...  167 us
    pallas_call x1, Pallas kernels, gather_weights(): pl.pallas_call(gather_kernel, out_shape=(jax.ShapeDtypeStruct((12, 2, 4,...  146 us
    dot_general x2, matrix products, one_block(): jnp.einsum('qhd,khd->hqk', grad_blk, value_heads, preferred_element_type=...  28.2 us
    convert_element_type x2, other arithmetic, one_block(): grad_scores = (probs * (grad_probs - inner)).astype(jnp.bfloat16)  22.5 us
    dot_general x2, matrix products, one_block(): jnp.einsum('hqk,qhd->khd', probs.astype(jnp.bfloat16), grad_blk, preferre...  19.5 us
    dot_general x2, matrix products, block_scores(): jnp.einsum('qhd,khd->hqk', query_blk, key_heads, preferred_element_type=j...  17.3 us
    reduce_sum x2, other arithmetic, one_block(): totals = jnp.sum(powers, axis=-1, keepdims=True)  16.6 us
    dot_general x2, matrix products, one_block(): jnp.einsum('hqk,khd->qhd', weights, value_heads, preferred_element_type=j...  15.8 us

profile of v1, /device:TPU:4, one launch (start us, length us, event | category | flops | bytes accessed | tf_op | source)
XLA Modules:
  0.0 654.9 jit_solution(5958026643599555573)
XLA Ops:
  2.5 1.4 reduce.2
  6.4 146.3 %shard_map.178 = (bf16[12,2,4,2,2,32,1024]{6,5,4,3,2,1,0:T(8,128)(2,1)}, bf16[4,2,4,2,2,128,256]{6,5,4,3,2,1,0:T(8,128)(2,1)}, bf16[2,4,2,2,16,128]{5,4,3,2,1,0:T(8,128)(2,1)}) custom-call(bf16[6,32,1024]{2,1,0:T(8,128)(2,1)} %proj_in.1, bf16[2,32,1024]{2,1,0:T(8,128)(2,1)} %proj_out.1, bf16[32,4096]{1,0:T(8,128)(2,1)} %ffn_in.1, bf16[128,1024]{1,0:T(8,128)(2,1)} %ffn_out.1, ...), custom_call_target="tpu_custom_call" | custom-call | tf_op jit(solution)/shard_map/pallas_call | solution.py:672
  153.7 2.6 slice.146
  156.4 2.5 convert_bitcast_fusion.1
  158.9 1.5 fusion.63
  160.4 3.5 slice.136
  163.9 13.4 %fusion.60 = (bf16[1,2,4,2,2,32,1024]{6,5,4,3,2,1,0:T(8,128)(2,1)}, bf16[1,2,4,2,2,32,1024]{6,5,4,3,2,1,0:T(8,128)(2,1)}, bf16[1,2,4,2,2,32,1024]{6,5,4,3,2,1,0:...) fusion(bf16[12,2,4,2,2,32,1024]{6,5,4,3,2,1,0:T(8,128)(2,1)} %g, ...), kind=kLoop, calls=%fused_computation.146 | loop fusion | bytes 29360128 | tf_op jit(solution)/shard_map/slice | solution.py:806
  177.3 4.1 convert_bitcast_fusion
  181.6 3.7 fusion.61
  185.4 7.4 %fusion.67 = (f32[16,512]{1,0:T(8,128)S(1)}, f32[16,512,512]{1,2,0:T(8,128)}) fusion(bf16[512,16,64]{0,2,1:T(8,128)(2,1)S(1)} %bitcast.178, bf16[512,16,64]{0,2,1:T(8,128)(2,1)S(1)} %bitcast.168, pred[512,512]{0,1:T(8,128)(4,1)S(1)} %get-tuple-element.187), kind=kOutput, calls=%fused_computation.153 | convolution fusion | flops 549445632 | bytes 19169280 | tf_op jit(solution)/shard_map/while/body/eval_jaxpr/qhd,khd->hqk/dot_general | solution.py:36
  192.8 8.3 %fusion = f32[16,512]{1,0:T(8,128)S(1)} fusion(f32[16,512,512]{1,2,0:T(8,128)} %get-tuple-element.189, f32[16,512]{1,0:T(8,128)S(1)} %get-tuple-element.188), kind=kLoop, calls=%fused_computation.12 | loop fusion | flops 8380416 | bytes 16842752 | tf_op jit(solution)/shard_map/while/body/eval_jaxpr/reduce_sum | solution.py:64
  201.7 7.7 %fusion.28 = bf16[16,64,512]{2,1,0:T(8,128)(2,1)S(1)} fusion(bf16[512,16,64]{0,2,1:T(8,128)(2,1)S(1)} %bitcast.195, f32[16,512,512]{1,2,0:T(8,128)} %get-tuple-element.189, f32[16,512]{1,0:T(8,128)S(1)} %fusion, f32[16,512]{1,0:T(8,128)S(1)} %get-tuple-element.188), kind=kOutput, calls=%fused_computation.84 | convolution fusion | flops 549978112 | bytes 18939904 | tf_op jit(solution)/shard_map/while/body/eval_jaxpr/hqk,khd->qhd/dot_general | solution.py:66
  209.4 1.4 fusion.68
  211.8 1.4 copy-done.22
  213.2 2.3 convolution_convert_fusion.4
  215.5 2.5 copy.77
  218.0 9.9 %fusion.69 = (f32[16,512]{1,0:T(8,128)S(1)}, f32[16,512,512]{1,2,0:T(8,128)}) fusion(bf16[512,16,64]{0,2,1:T(8,128)(2,1)} %bitcast.172, bf16[512,16,64]{0,2,1:T(8,128)(2,1)} %bitcast.170, pred[512,512]{0,1:T(8,128)(4,1)S(1)} %get-tuple-element.186), kind=kOutput, calls=%fused_computation.155 | convolution fusion | flops 549445632 | bytes 19169280 | tf_op jit(solution)/shard_map/while/body/eval_jaxpr/qhd,khd->hqk/dot_general | solution.py:36
  227.9 8.4 %fusion.1 = f32[16,512]{1,0:T(8,128)S(1)} fusion(f32[16,512,512]{1,2,0:T(8,128)} %get-tuple-element.193, f32[16,512]{1,0:T(8,128)S(1)} %get-tuple-element.192), kind=kLoop, calls=%fused_computation.13 | loop fusion | flops 8380416 | bytes 16842752 | tf_op jit(solution)/shard_map/while/body/eval_jaxpr/reduce_sum | solution.py:64
  236.3 8.1 %fusion.27 = bf16[16,64,512]{2,1,0:T(8,128)(2,1)S(1)} fusion(bf16[512,16,64]{0,2,1:T(8,128)(2,1)S(1)} %bitcast.198, f32[16,512,512]{1,2,0:T(8,128)} %get-tuple-element.193, f32[16,512]{1,0:T(8,128)S(1)} %fusion.1, f32[16,512]{1,0:T(8,128)S(1)} %get-tuple-element.192), kind=kOutput, calls=%fused_computation.83 | convolution fusion | flops 549978112 | bytes 18939904 | tf_op jit(solution)/shard_map/while/body/eval_jaxpr/hqk,khd->qhd/dot_general | solution.py:66
  244.5 1.5 fusion.70
  247.0 1.4 copy-done.29
  249.3 7.8 %fusion.36 = f32[512,4096]{1,0:T(8,128)} fusion(bf16[1024,1024]{1,0:T(8,128)(2,1)S(1)} %bitcast.208, bf16[1024,1024]{1,0:T(8,128)(2,1)S(1)} %bitcast.210, bf16[1024,1024]{1,0:T(8,128)(2,1)S(1)} %bitcast.212, bf16[1024,1024]{1,0:T(8,128)(2,1)S(1)} %bitcast.205, f32[512,1024]{1,0:T(8,128)S(1)} %get-tuple-element.195, f32[1024]{0:T(1024)S(1)} %bitcast.244, ...), kind=kOutput, calls=%fused_computation.91 | convolution fusion | flops 4331143168 | bytes 18886656 | tf_op jit(solution)/shard_map/dot_general | solution.py:153
  257.1 10.2 %fusion.71 = (f32[512]{0:T(512)S(1)}, f32[512,1024]{1,0:T(8,128)S(1)}) fusion(bf16[4096,256]{1,0:T(8,128)(2,1)} %bitcast.215, bf16[4096,256]{1,0:T(8,128)(2,1)} %bitcast.217, bf16[4096,256]{1,0:T(8,128)(2,1)} %bitcast.219, bf16[4096,256]{1,0:T(8,128)(2,1)} %bitcast.213, f32[512,4096]{1,0:T(8,128)} %fusion.36, f32[1024]{0:T(1024)S(1)} %bitcast.245, ...), kind=kOutput, calls=%fused_computation.157 | convolution fusion | flops 4351065600 | bytes 20985856 | tf_op jit(solution)/shard_map/dot_general | solution.py:155
  269.4 2.5 fusion.59
  271.9 14.3 %fusion.10 = bf16[512,4096]{1,0:T(8,128)(2,1)} fusion(f32[512,4096]{1,0:T(8,128)} %fusion.36, bf16[4096,256]{1,0:T(8,128)(2,1)} %bitcast.216, bf16[4096,256]{1,0:T(8,128)(2,1)} %bitcast.218, bf16[4096,256]{1,0:T(8,128)(2,1)} %bitcast.220, bf16[4096,256]{1,0:T(8,128)(2,1)} %bitcast.214, f32[512,1024]{1,0:T(8,128)} %get-tuple-element.142, ...), kind=kOutput, calls=%fused_computation.24 | convolution fusion | flops 4371513344 | bytes 23070720 | tf_op jit(solution)/shard_map/td,fd->tf/dot_general | solution.py:188
  286.3 10.1 %multiply_reduce_fusion.2 = (bf16[1024]{0:T(1024)(128)(2,1)S(1)}, f32[512]{0:T(512)S(1)}, bf16[1024]{0:T(1024)(128)(2,1)S(1)}, f32[512,1024]{1,0:T(8,128)}) fusion(f32[512,1024]{1,0:T(8,128)S(1)} %get-tuple-element.195, f32[512]{0:T(512)S(1)} %fusion.43, f32[512]{0:T(512)S(1)} %broadcast_multiply_fusion.1, f32[1024]{0:T(1024)S(1)} %bitcast.236, ...), kind=kOutput, calls=%fused_computation.58 | convolution fusion | flops 4334286336 | bytes 18890752 | tf_op jit(solution)/shard_map/tf,df->td/dot_general | solution.py:194
  296.4 9.3 %convolution_convert_fusion = bf16[4096,1024]{0,1:T(8,128)(2,1)} fusion(f32[512,1024]{1,0:T(8,128)S(1)} %copy-done.30, f32[512]{0:T(512)S(1)} %negate_multiply_fusion.2, f32[512,4096]{1,0:T(8,128)} %fusion.36), kind=kOutput, calls=%fused_computation.36 | convolution fusion | flops 4319084544 | bytes 18876416 | tf_op jit(solution)/shard_map/tf,td->fd/dot_general | solution.py:185
  305.6 12.1 %copy.95 = bf16[4096,4,256]{2,0,1:T(8,128)(2,1)} copy(bf16[4096,4,256]{0,2,1:T(8,128)(2,1)} %bitcast.185) | data formatting | bytes 16777216 | tf_op jit(solution)/shard_map/reshape | solution.py:826
  317.8 2.4 fusion.58
  320.2 1.4 copy-done.31
  321.6 1.3 convolution_convert_fusion.3
  323.7 9.8 %fusion.29 = bf16[16,64,512]{2,1,0:T(8,128)(2,1)} fusion(bf16[512,16,64]{0,2,1:T(8,128)(2,1)S(1)} %bitcast.176, f32[16,512,512]{1,2,0:T(8,128)} %get-tuple-element.193, f32[16,512]{1,0:T(8,128)S(1)} %log_add_fusion.1), kind=kOutput, calls=%fused_computation.88 | convolution fusion | flops 545783808 | bytes 18907136 | tf_op jit(solution)/shard_map/while/body/eval_jaxpr/hqk,qhd->khd/dot_general | solution.py:95
  333.5 2.4 copy.91
  335.9 9.1 %convolution_convert_fusion.1 = bf16[1024,4096]{1,0:T(8,128)(2,1)} fusion(bf16[512,4096]{1,0:T(8,128)(2,1)} %fusion.10, f32[512,1024]{1,0:T(8,128)S(1)} %copy-done.15, f32[1024]{0:T(1024)S(1)} %bitcast.246, f32[1024]{0:T(1024)S(1)} %bitcast.238, f32[512]{0:T(512)S(1)} %fusion.43, f32[512]{0:T(512)S(1)} %broadcast_multiply_fusion.1), kind=kOutput, calls=%fused_computation.37 | convolution fusion | flops 4301783040 | bytes 14692352 | tf_op jit(solution)/shard_map/td,tf->df/dot_general | solution.py:191
  345.1 16.6 %multiply_reduce_fusion.1 = (f32[16,512]{1,0:T(8,128)}, f32[16,512,512]{1,2,0:T(8,128)}) fusion(f32[16,512,512]{1,2,0:T(8,128)} %get-tuple-element.193, f32[16,512]{1,0:T(8,128)} %copy-done.49, bf16[512,16,64]{0,2,1:T(8,128)(2,1)} %bitcast.177, bf16[512,16,64]{0,2,1:T(8,128)(2,1)} %bitcast.197), kind=kOutput, calls=%fused_computation.4 | convolution fusion | flops 549445632 | bytes 35717120 | tf_op jit(solution)/shard_map/while/body/eval_jaxpr/qhd,khd->hqk/dot_general | solution.py:98
  361.7 10.5 %multiply_convert_fusion.1 = bf16[16,512,512]{1,2,0:T(8,128)(2,1)} fusion(f32[16,512,512]{1,2,0:T(8,128)} %get-tuple-element.200, f32[16,512,512]{1,2,0:T(8,128)S(1)} %bitcast.166, f32[16,512]{1,0:T(8,128)} %get-tuple-element.199, f32[16,512]{1,0:T(8,128)} %copy-done.49), kind=kLoop, calls=%fused_computation.3 | loop fusion | flops 16777216 | bytes 42008576 | tf_op jit(solution)/shard_map/while/body/eval_jaxpr/convert_element_type | solution.py:102
  372.2 6.5 multiply_convert_fusion.3
  378.7 2.5 multiply_convert_fusion.6
  381.2 1.7 copy.90
  383.0 6.3 bitcast_convert_fusion
  389.4 2.2 multiply_reduce_fusion.3
  392.3 1.3 copy-done.34
  393.7 2.3 convolution_convert_fusion.2
  395.9 2.3 copy.81
  399.2 9.8 %fusion.32 = bf16[16,64,512]{2,1,0:T(8,128)(2,1)} fusion(bf16[512,16,64]{0,2,1:T(8,128)(2,1)} %bitcast.174, f32[16,512,512]{1,2,0:T(8,128)} %get-tuple-element.189, f32[16,512]{1,0:T(8,128)S(1)} %copy-done.48), kind=kOutput, calls=%fused_computation.89 | convolution fusion | flops 545783808 | bytes 18907136 | tf_op jit(solution)/shard_map/while/body/eval_jaxpr/hqk,qhd->khd/dot_general | solution.py:95
  408.9 2.3 copy.87
  411.2 11.6 %multiply_reduce_fusion = (f32[16,512]{1,0:T(8,128)S(1)}, f32[16,512,512]{1,2,0:T(8,128)}) fusion(f32[16,512,512]{1,2,0:T(8,128)} %get-tuple-element.189, f32[16,512]{1,0:T(8,128)S(1)} %copy-done.48, bf16[512,16,64]{0,2,1:T(8,128)(2,1)} %bitcast.175, bf16[512,16,64]{0,2,1:T(8,128)(2,1)} %bitcast.196), kind=kOutput, calls=%fused_computation.1 | convolution fusion | flops 549445632 | bytes 35717120 | tf_op jit(solution)/shard_map/while/body/eval_jaxpr/qhd,khd->hqk/dot_general | solution.py:98
  422.8 12.0 %multiply_convert_fusion = bf16[16,512,512]{1,2,0:T(8,128)(2,1)S(1)} fusion(f32[16,512,512]{1,2,0:T(8,128)} %get-tuple-element.203, f32[16,512,512]{1,2,0:T(8,128)} %get-tuple-element.189, f32[16,512]{1,0:T(8,128)S(1)} %get-tuple-element.202, f32[16,512]{1,0:T(8,128)S(1)} %copy-done.48), kind=kLoop, calls=%fused_computation | loop fusion | flops 16777216 | bytes 42008576 | tf_op jit(solution)/shard_map/while/body/eval_jaxpr/convert_element_type | solution.py:102
  434.8 3.6 multiply_convert_fusion.4
  438.4 2.4 multiply_convert_fusion.5
  440.9 2.3 copy.85
  443.1 2.3 copy.86
  445.4 8.9 %fusion.24 = bf16[512,1024]{1,0:T(8,128)(2,1)} fusion(f32[512,1024]{1,0:T(8,128)} %copy-done.34, bf16[3,1024,1024]{2,1,0:T(8,128)(2,1)} %bitcast.188, bf16[1,512,1024]{2,1,0:T(8,128)(2,1)} %copy.87, bf16[1,512,1024]{2,1,0:T(8,128)(2,1)} %copy.86, bf16[1,512,1024]{2,1,0:T(8,128)(2,1)} %copy.85, f32[512]{0:T(512)S(1)} %negate_multiply_fusion), kind=kOutput, calls=%fused_computation.57 | convolution fusion | flops 3226468352 | bytes 12584960 | tf_op jit(solution)/shard_map/wte,wde->td/dot_general | solution.py:258
  454.4 5.7 bitcast_dynamic-update-slice_fusion
  460.1 2.9 bitcast_dynamic-update-slice_fusion.4
  463.0 4.4 bitcast_dynamic-update-slice_fusion.1
  467.3 2.7 bitcast_dynamic-update-slice_fusion.3
  470.0 2.6 bitcast_dynamic-update-slice_fusion.2
  472.7 7.9 %fusion.15 = bf16[12,1024,1024]{2,1,0:T(8,128)(2,1)} fusion(bf16[12,1024,1024]{2,1,0:T(8,128)(2,1)} %bitcast_dynamic-update-slice_fusion.2, bf16[128,4,8,1024]{3,2,1,0:T(8,128)(2,1)} %bitcast.182), kind=kLoop, calls=%fused_computation.28 | loop fusion | bytes 16777216 | tf_op jit(solution)/shard_map/concatenate | solution.py:818
  480.6 167.2 %shard_map.179 = (f32[12,32,1024]{2,1,0:T(8,128)}, f32[128,1024]{1,0:T(8,128)}, f32[16,128]{1,0:T(8,128)}) custom-call(bf16[12,2,4,2,2,32,1024]{6,5,4,3,2,1,0:T(8,128)(2,1)} %bitcast.67.refs_0_, bf16[4,2,4,2,2,128,256]{6,5,4,3,2,1,0:T(8,128)(2,1)} %bitcast.167, bf16[2,4,2,2,16,128]{5,4,3,2,1,0:T(8,128)(2,1)} %broadcast_in_dim.169.refs_2_), custom_call_target="tpu_custom_call" | custom-call | tf_op jit(solution)/shard_map/pallas_call | solution.py:766
  647.8 1.5 fusion.66
  649.3 1.7 slice.165
  651.0 1.1 slice_bitcast_fusion
  652.1 0.9 slice.164
  (183 shorter events, 15.3 us)
Async XLA Ops:
  0.6 155.7 %copy-start = (bf16[512,1024]{1,0:T(8,128)(2,1)S(1)}, bf16[512,1024]{1,0:T(8,128)(2,1)}, u32[]{:S(2)}) copy-start(bf16[512,1024]{1,0:T(8,128)(2,1)} %param.12) | copy-start | bytes 3145732
  153.7 90.7 %copy-start.55 = (f32[1,8,128]{2,0,1:T(1,128)}, f32[1,8,128]{2,0,1:T(1,128)S(1)}, u32[]{:S(2)}) copy-start(f32[1,8,128]{2,0,1:T(1,128)S(1)} %get-tuple-element.176) | copy-start | bytes 12292
  153.7 90.7 %copy-start.59 = (f32[1,8,128]{2,0,1:T(1,128)}, f32[1,8,128]{2,0,1:T(1,128)S(1)}, u32[]{:S(2)}) copy-start(f32[1,8,128]{2,0,1:T(1,128)S(1)} %get-tuple-element.206) | copy-start | bytes 12292
  156.4 2.5 copy-start.17
  163.9 13.4 %copy-start.16 = (bf16[3,2,4,2,2,32,1024]{6,5,4,3,2,1,0:T(8,128)(2,1)}, bf16[3,2,4,2,2,32,1024]{6,5,4,3,2,1,0:T(8,128)(2,1)S(1)}, u32[]{:S(2)}) copy-start(bf16[3,2,4,2,2,32,1024]{6,5,4,3,2,1,0:T(8,128)(2,1)S(1)} %slice.136) | copy-start | bytes 18874372
  163.9 13.4 %copy-start.42 = (bf16[512,1024]{1,0:T(8,128)(2,1)S(1)}, bf16[512,1024]{1,0:T(8,128)(2,1)}, u32[]{:S(2)}) copy-start(bf16[512,1024]{1,0:T(8,128)(2,1)} %param.11) | copy-start | bytes 3145732
  177.2 4.4 slice-start.4
  177.3 4.4 slice-start.5
  181.6 3.7 copy-start.4
  181.6 3.8 copy-start.8
  181.6 20.1 %copy-start.18 = (bf16[1,512,1024]{1,2,0:T(8,128)(2,1)}, bf16[1,512,1024]{1,2,0:T(8,128)(2,1)S(1)}, u32[]{:S(2)}) copy-start(bf16[1,512,1024]{1,2,0:T(8,128)(2,1)S(1)} %get-tuple-element.168) | copy-start | bytes 3145732
  201.7 7.7 %copy-start.11 = (bf16[1,2,4,2,2,32,1024]{6,5,4,3,2,1,0:T(8,128)(2,1)S(1)}, bf16[1,2,4,2,2,32,1024]{6,5,4,3,2,1,0:T(8,128)(2,1)}, u32[]{:S(2)}) copy-start(bf16[1,2,4,2,2,32,1024]{6,5,4,3,2,1,0:T(8,128)(2,1)} %get-tuple-element.161) | copy-start | bytes 6291460
  201.7 7.7 %copy-start.43 = (bf16[512,1024]{1,0:T(8,128)(2,1)S(1)}, bf16[512,1024]{1,0:T(8,128)(2,1)}, u32[]{:S(2)}) copy-start(bf16[512,1024]{1,0:T(8,128)(2,1)} %param.11) | copy-start | bytes 3145732
  210.8 33.6 %copy-start.2 = (f32[512,1024]{1,0:T(8,128)}, f32[512,1024]{1,0:T(8,128)S(1)}, u32[]{:S(2)}) copy-start(f32[512,1024]{1,0:T(8,128)S(1)} %get-tuple-element.191) | copy-start | bytes 6291460
  210.8 2.4 copy-start.22
  210.8 33.6 %copy-start.50 = (f32[512]{0:T(512)}, f32[512]{0:T(512)S(1)}, u32[]{:S(2)}) copy-start(f32[512]{0:T(512)S(1)} %broadcast_multiply_fusion.2) | copy-start | bytes 6148
  213.2 31.3 %copy-start.57 = (f32[512]{0:T(512)}, f32[512]{0:T(512)S(1)}, u32[]{:S(2)}) copy-start(f32[512]{0:T(512)S(1)} %fusion.42) | copy-start | bytes 6148
  227.9 8.4 %copy-start.19 = (bf16[1,512,1024]{1,2,0:T(8,128)(2,1)S(1)}, bf16[1,512,1024]{1,2,0:T(8,128)(2,1)}, u32[]{:S(2)}) copy-start(bf16[1,512,1024]{1,2,0:T(8,128)(2,1)} %get-tuple-element.171) | copy-start | bytes 3145732
  236.3 87.4 %copy-start.49 = (f32[16,512]{1,0:T(8,128)}, f32[16,512]{1,0:T(8,128)S(1)}, u32[]{:S(2)}) copy-start(f32[16,512]{1,0:T(8,128)S(1)} %log_add_fusion.1) | copy-start | bytes 98308
  236.3 8.2 %copy-start.24 = (bf16[1,2,4,2,2,32,1024]{6,5,4,3,2,1,0:T(8,128)(2,1)S(1)}, bf16[1,2,4,2,2,32,1024]{6,5,4,3,2,1,0:T(8,128)(2,1)}, u32[]{:S(2)}) copy-start(bf16[1,2,4,2,2,32,1024]{6,5,4,3,2,1,0:T(8,128)(2,1)} %get-tuple-element.147) | copy-start | bytes 6291460
  244.5 2.0 copy-start.27
  244.5 2.5 copy-start.28
  244.5 3.9 copy-start.29
  246.0 40.2 %copy-start.13 = (f32[512,1024]{1,0:T(8,128)}, f32[512,1024]{1,0:T(8,128)S(1)}, u32[]{:S(2)}) copy-start(f32[512,1024]{1,0:T(8,128)S(1)} %get-tuple-element.195) | copy-start | bytes 6291460
  246.1 3.2 copy-start.26
  286.3 10.1 %copy-start.30 = (f32[512,1024]{1,0:T(8,128)S(1)}, f32[512,1024]{1,0:T(8,128)}, u32[]{:S(2)}) copy-start(f32[512,1024]{1,0:T(8,128)} %get-tuple-element.142) | copy-start | bytes 6291460
  305.6 12.1 %copy-start.14 = (f32[512,1024]{1,0:T(8,128)S(1)}, f32[512,1024]{1,0:T(8,128)}, u32[]{:S(2)}) copy-start(f32[512,1024]{1,0:T(8,128)} %copy-done.13) | copy-start | bytes 6291460
  317.8 3.8 copy-start.25
  323.6 9.8 %copy-start.7 = (bf16[512,1024]{0,1:T(8,128)(2,1)}, bf16[512,1024]{0,1:T(8,128)(2,1)S(1)}, u32[]{:S(2)}) copy-start(bf16[512,1024]{0,1:T(8,128)(2,1)S(1)} %copy.79) | copy-start | bytes 3145732
  333.5 2.4 copy-start.15
  345.1 16.6 %slice-start = ((s8[16777216]{0:T(1024)(128)(4,1)}), s8[4194304]{0:T(1024)(128)(4,1)S(1)}, s32[]{:S(2)}) async-start(s8[16777216]{0:T(1024)(128)(4,1)} %bitcast.165), calls=%async_computation | async-start | bytes 8388608
  345.1 16.6 %slice-start.1 = ((s8[16777216]{0:T(1024)(128)(4,1)}), s8[4194304]{0:T(1024)(128)(4,1)S(1)}, s32[]{:S(2)}) async-start(s8[16777216]{0:T(1024)(128)(4,1)} %bitcast.165), calls=%async_computation.1 | async-start | bytes 8388608
  345.1 16.6 %slice-start.2 = ((s8[16777216]{0:T(1024)(128)(4,1)}), s8[4194304]{0:T(1024)(128)(4,1)S(1)}, s32[]{:S(2)}) async-start(s8[16777216]{0:T(1024)(128)(4,1)} %bitcast.165), calls=%async_computation.2 | async-start | bytes 8388608
  345.1 16.6 %slice-start.3 = ((s8[16777216]{0:T(1024)(128)(4,1)}), s8[4194304]{0:T(1024)(128)(4,1)S(1)}, s32[]{:S(2)}) async-start(s8[16777216]{0:T(1024)(128)(4,1)} %bitcast.165), calls=%async_computation.3 | async-start | bytes 8388608
  372.2 6.5 copy-start.1
  372.2 6.5 copy-start.6
  382.9 6.4 copy-start.3
  382.9 6.4 copy-start.20
  382.9 6.4 copy-start.23
  382.9 6.4 copy-start.32
  382.9 6.4 copy-start.51
  383.0 6.4 copy-start.56
  383.0 6.4 copy-start.58
  383.0 6.4 copy-start.62
  389.4 2.2 copy-start.53
  391.6 2.1 copy-start.12
  395.9 2.3 copy-start.54
  395.9 3.2 copy-start.48
  422.8 12.0 %copy-start.9 = (bf16[1,512,1024]{1,2,0:T(8,128)(2,1)S(1)}, bf16[1,512,1024]{1,2,0:T(8,128)(2,1)}, u32[]{:S(2)}) copy-start(bf16[1,512,1024]{1,2,0:T(8,128)(2,1)} %copy-done.8) | copy-start | bytes 3145732
  434.8 3.6 copy-start.5
  445.4 8.9 %copy-start.39 = (bf16[1,512,1024]{2,1,0:T(8,128)(2,1)S(1)}, bf16[1,512,1024]{2,1,0:T(8,128)(2,1)}, u32[]{:S(2)}) copy-start(bf16[1,512,1024]{2,1,0:T(8,128)(2,1)} %copy.87) | copy-start | bytes 3145732
  445.4 8.9 %copy-start.40 = (bf16[1,512,1024]{2,1,0:T(8,128)(2,1)S(1)}, bf16[1,512,1024]{2,1,0:T(8,128)(2,1)}, u32[]{:S(2)}) copy-start(bf16[1,512,1024]{2,1,0:T(8,128)(2,1)} %copy.85) | copy-start | bytes 3145732
  445.4 8.9 %copy-start.41 = (bf16[1,512,1024]{2,1,0:T(8,128)(2,1)S(1)}, bf16[1,512,1024]{2,1,0:T(8,128)(2,1)}, u32[]{:S(2)}) copy-start(bf16[1,512,1024]{2,1,0:T(8,128)(2,1)} %copy.86) | copy-start | bytes 3145732
  445.4 8.9 %copy-start.44 = (bf16[512,1024]{1,0:T(8,128)(2,1)S(1)}, bf16[512,1024]{1,0:T(8,128)(2,1)}, u32[]{:S(2)}) copy-start(bf16[512,1024]{1,0:T(8,128)(2,1)} %param.11) | copy-start | bytes 3145732
  454.3 5.7 copy-start.21
  454.3 5.7 copy-start.60
  460.0 2.9 copy-start.37
  460.1 2.9 copy-start.38
  463.0 4.4 copy-start.35
  463.0 4.4 copy-start.46
  467.3 2.7 copy-start.33
  467.3 2.7 copy-start.64
  647.8 4.3 copy-start.36
  649.3 4.6 copy-start.47
  (7 other events, 8.9 us)
